TPU v7x, 128 devices: a whole 4x4x4 slice. The times are simulated.
128 devices in a mesh: dp: 4 (over x), tensor: 2 (over core), expert: 16 (over z, y).
Axes of the slice: x: 4, y: 4, z: 4, core: 2. Of those that a mesh axis runs over, the one named last changes fastest.
Arguments:
- tokens: bfloat16 [8192, 2304], P(('dp', 'tensor', 'expert')), may hold values from -6 to 6
- routes: int32 [8192, 2], P(('dp', 'tensor', 'expert')), may hold values from 0 to 7, all different within a row; in each aligned block of 64 rows (0 to 63, 64 to 127, ...) at most 24 rows name the same one
- gates: float32 [8192, 2], P(('dp', 'tensor', 'expert')), may hold values from 0.2 to 1
- segments: int32 [8192], P(('dp', 'tensor', 'expert')), may hold values from 0 to 31, never falling along the last dimension, each value on 1 to 512 neighbouring positions
- w_gate: bfloat16 [16, 2304, 3840], P('expert', None, ('dp', 'tensor')), may hold values from -0.125 to 0.125
- w_up: bfloat16 [16, 2304, 3840], P('expert', None, ('dp', 'tensor')), may hold values from -0.125 to 0.125
- w_down: bfloat16 [16, 3840, 2304], P('expert', ('dp', 'tensor')), may hold values from -0.0625 to 0.0625
Outputs:
- embedded: bfloat16 [8192, 2304], P(('dp', 'tensor', 'expert'))
- pooled: float32 [32, 2304], replicated
Inputs may be any that keep to these rules, and one draw needn't show every extreme that they name: `routes`: each residue names two different experts. Within the rows of one device no expert is named more than 24 times, and in every draw some expert is named exactly 24 times by the rows of some device. `segments`: sequence numbers never fall along the residues; each sequence has 1 to 512 residues and one has exactly 512.
All inputs are finite; a program needn't handle non-finite values.
Results may differ from a plain program's by a relative error of at most 0.0085.
Values may be sent and summed in bfloat16 or wider, within the bound.
A program may use at most 64 MiB of HBM per device.

v0:
```python
import jax
import jax.numpy as jnp
from jax import lax
from jax.sharding import PartitionSpec as P

EXPERTS = 8
TOP = 2
CAP = 24
epsilon = 1e-06


def norm_tokens(tokens):
    values = tokens.astype(jnp.float32)
    scale = lax.rsqrt(jnp.mean(values * values, axis=1, keepdims=True) + epsilon)
    return (values, (values * scale).astype(jnp.bfloat16))


def slot_numbers(routes):
    flat_routes = routes.reshape(-1)
    onehot = (flat_routes[:, None] == jnp.arange(EXPERTS, dtype=jnp.int32)[None, :]).astype(
        jnp.int32
    )
    before = jnp.cumsum(onehot, axis=0) - onehot
    slot_rank = jnp.sum(before * onehot, axis=1)
    return flat_routes * CAP + slot_rank


def placement_matrix(slot_index, tok_count):
    hits = (jnp.arange(EXPERTS * CAP, dtype=jnp.int32)[:, None] == slot_index[None, :]).astype(
        jnp.int32
    )
    return jnp.sum(hits.reshape(EXPERTS * CAP, tok_count, TOP), axis=2).astype(jnp.bfloat16)


def fan_out(slot_rows, replicas):
    leading = slot_rows.shape[:-2]
    features = slot_rows.shape[-1]
    shaped = slot_rows.reshape(leading + (EXPERTS, CAP, features))
    shaped = jnp.repeat(shaped, replicas, axis=len(leading))
    return shaped.reshape(leading + (EXPERTS * replicas * CAP, features))


def expert_hidden(row_block, w_gate, w_up):
    gate_proj = jnp.einsum("nacd,adf->nacf", row_block, w_gate, preferred_element_type=jnp.float32)
    up_proj = jnp.einsum("nacd,adf->nacf", row_block, w_up, preferred_element_type=jnp.float32)
    return (jax.nn.silu(gate_proj) * up_proj).astype(jnp.bfloat16)


def shards(tokens, routes, gates, segments, w_gate, w_up, w_down):
    tok_count = tokens.shape[0]
    width = tokens.shape[1]
    experts_axis = lax.axis_size("expert")
    per_device = w_gate.shape[0]
    replicas = max(1, experts_axis // EXPERTS)
    plane = lax.axis_size("dp") * lax.axis_size("tensor")
    values, normed = norm_tokens(tokens)
    slot_index = slot_numbers(routes)
    placing = placement_matrix(slot_index, tok_count)
    slot_rows = jnp.dot(placing, normed, preferred_element_type=jnp.float32).astype(jnp.bfloat16)
    send_rows = fan_out(slot_rows, replicas)
    received = lax.all_to_all(send_rows, "expert", split_axis=0, concat_axis=0, tiled=True)
    local_rows = received.reshape(experts_axis, per_device, CAP, width)
    hidden = expert_hidden(
        lax.all_gather(local_rows, ("dp", "tensor"), axis=0, tiled=True), w_gate, w_up
    )
    summed = lax.psum_scatter(
        jnp.einsum("nacf,afd->nacd", hidden, w_down, preferred_element_type=jnp.float32).astype(
            jnp.bfloat16
        ),
        ("dp", "tensor"),
        scatter_dimension=0,
        tiled=True,
    )
    returned = lax.all_to_all(summed, "expert", split_axis=0, concat_axis=0, tiled=True).astype(
        jnp.float32
    )
    expert_out = jnp.sum(returned.reshape(EXPERTS, replicas, CAP, width), axis=1)
    picked = jnp.take(expert_out.reshape(EXPERTS * CAP, width), slot_index, axis=0).reshape(
        tok_count, TOP, width
    )
    mixed = values + jnp.sum(gates[:, :, None] * picked, axis=1)
    embedded = mixed.astype(jnp.bfloat16)
    devices_all = plane * experts_axis
    seq_total = tok_count * devices_all // 256
    seq_hot = (jnp.arange(seq_total, dtype=jnp.int32)[:, None] == segments[None, :]).astype(
        jnp.bfloat16
    )
    seq_sums = jnp.dot(seq_hot, embedded, preferred_element_type=jnp.float32)
    seq_counts = jnp.sum(seq_hot.astype(jnp.float32), axis=1)
    total_sums, total_counts = lax.psum((seq_sums, seq_counts), ("dp", "tensor", "expert"))
    pooled = total_sums / total_counts[:, None]
    return (embedded, pooled)


def solution(mesh):
    placed = (
        P(("dp", "tensor", "expert"), None),
        P(("dp", "tensor", "expert"), None),
        P(("dp", "tensor", "expert"), None),
        P(("dp", "tensor", "expert")),
        P("expert", None, ("dp", "tensor")),
        P("expert", None, ("dp", "tensor")),
        P("expert", ("dp", "tensor"), None),
    )
    return jax.shard_map(
        shards,
        mesh=mesh,
        in_specs=placed,
        out_specs=(P(("dp", "tensor", "expert"), None), P()),
        check_vma=False,
    )
```

profile of v0, /device:TPU:1, one launch (start us, length us, event | category | flops | bytes accessed | tf_op | source)
XLA Modules:
  0.0 430.2 jit_solution(17965702247409334811)
XLA Ops:
  7.2 0.0 copy-start
  7.2 0.0 all-gather.3.cloned.1.call-start
  7.2 0.9 copy.33
  8.1 0.1 reshape.117
  8.3 0.1 fusion.14
  8.4 0.2 reduce_window_sum.11
  8.5 0.2 select_reduce_fusion
  8.7 0.1 reduce_sum.59
  8.9 0.1 copy.34
  8.9 0.7 compare_and_fusion
  9.6 0.1 convert_reduce_fusion.1
  9.7 1.1 fusion.9
  10.9 1.4 convolution_convert_fusion
  12.3 0.1 broadcast_in_dim.13
  12.4 32.4 %all_to_all.14 = bf16[16,24,2304]{2,1,0:T(8,128)(2,1)S(1)} all-to-all(bf16[16,24,2304]{2,1,0:T(8,128)(2,1)S(1)} %bitcast.63), channel_id=1, replica_groups=mesh['dp'=4,'tensor'=2,'expert'=16] {'expert'}, dimensions={0} | all-to-all | bytes 3538944 | tf_op jit(solution)/shard_map/all_to_all | solution.py:61
  44.8 1.5 copy.36
  46.3 0.0 all-gather.3.cloned.1.call-update
  46.3 0.0 reduce-scatter.2.cloned.1.call-start
  46.4 73.1 %all-gather.3.cloned.1.call-done = bf16[128,24,2304]{2,0,1:T(8,128)(2,1)} async-done(((bf16[16,24,2304]{2,0,1:T(8,128)(2,1)}), bf16[128,24,2304]{2,0,1:T(8,128)(2,1)}) %all-gather.3.cloned.1.call-update) | async-done | bytes 14155792 | tf_op jit(solution)/shard_map/all_gather | solution.py:64
  119.5 11.4 %fusion.6 = f32[128,24,480]{0,2,1:T(8,128)S(1)} fusion(bf16[128,24,2304]{2,0,1:T(8,128)(2,1)} %all-gather.3.cloned.1.call-done, bf16[1,2304,480]{1,2,0:T(8,128)(2,1)} %param.12), kind=kOutput, calls=%fused_computation.13 | convolution fusion | flops 6794772480 | bytes 22265856 | tf_op jit(solution)/shard_map/nacd,adf->nacf/dot_general | solution.py:45
  130.9 0.0 copy-done.5
  130.9 0.0 copy-done.6
  130.9 8.1 %fusion = bf16[128,1,24,480]{0,3,2,1:T(8,128)(2,1)S(1)} fusion(f32[128,24,480]{0,2,1:T(8,128)S(1)} %fusion.6, bf16[128,24,2304]{2,0,1:T(8,128)(2,1)S(1)} %copy-done.5, bf16[1,2304,480]{1,2,0:T(8,128)(2,1)S(1)} %copy-done.6), kind=kOutput, calls=%fused_computation.3 | convolution fusion | flops 6803619840 | bytes 25214976 | tf_op jit(solution)/shard_map/nacd,adf->nacf/dot_general | solution.py:44
  139.0 0.0 copy-done
  139.0 10.3 %convert_bitcast_fusion = bf16[128,1,24,2304]{3,0,2,1:T(8,128)(2,1)} fusion(bf16[128,1,24,480]{0,3,2,1:T(8,128)(2,1)S(1)} %fusion, bf16[1,480,2304]{2,1,0:T(8,128)(2,1)S(1)} %copy-done), kind=kOutput, calls=%fused_computation.1 | convolution fusion | flops 6801850368 | bytes 19316736 | tf_op jit(solution)/shard_map/nacf,afd->nacd/dot_general | solution.py:67
  149.2 0.0 reduce-scatter.2.cloned.1.call-update
  149.3 79.5 %reduce-scatter.2.cloned.1.call-done = bf16[16,1,24,2304]{3,0,2,1:T(8,128)(2,1)} async-done(((bf16[128,1,24,2304]{3,0,2,1:T(8,128)(2,1)}), bf16[16,1,24,2304]{3,0,2,1:T(8,128)(2,1)}) %reduce-scatter.2.cloned.1.call-update) | async-done | bytes 1769488 | tf_op jit(solution)/shard_map/reduce_scatter | solution.py:66
  228.8 3.2 copy.37
  232.0 6.9 %all-to-all-start.1 = ((bf16[16,1,24,2304]{3,2,1,0:T(8,128)(2,1)}), bf16[16,1,24,2304]{3,2,1,0:T(8,128)(2,1)}, u32[]{:S(2)}, u32[]{:S(2)}) async-start(bf16[16,1,24,2304]{3,2,1,0:T(8,128)(2,1)} %copy.37), calls=%async_computation.2 | async-start | bytes 3538944 | tf_op jit(solution)/shard_map/all_to_all | solution.py:74
  238.9 0.2 all-reduce.2.cloned.1.call-start
  239.1 0.0 copy-done.2
  239.1 0.1 copy.40
  239.2 0.1 mul.61
  239.3 0.1 copy.35
  239.5 0.1 copy.32
  239.6 23.3 %all-to-all-done.1 = bf16[16,1,24,2304]{3,2,1,0:T(8,128)(2,1)} async-done(((bf16[16,1,24,2304]{3,2,1,0:T(8,128)(2,1)}), bf16[16,1,24,2304]{3,2,1,0:T(8,128)(2,1)}, u32[]{:S(2)}, u32[]{:S(2)}) %all-to-all-start.1) | async-done | bytes 1769504 | tf_op jit(solution)/shard_map/all_to_all | solution.py:74
  262.9 3.2 convert_reduce_fusion
  266.0 4.0 gather_fusion
  270.0 2.0 gather.7
  272.0 3.2 multiply_reduce_fusion
  275.3 1.0 fusion.11
  276.3 0.0 copy-start.1
  276.3 0.9 fusion.17
  277.2 0.0 all-reduce.2.cloned.1.call-update
  277.2 0.1 convert_reduce_fusion.2
  277.4 68.6 %psum.15 = f32[32]{0:T(128)S(1)} all-reduce(f32[32]{0:T(128)S(1)} %convert_reduce_fusion.2), channel_id=1, replica_groups=mesh['dp'=4,'tensor'=2,'expert'=16] {'dp','tensor','expert'}, use_global_device_ids=true, to_apply=%region_9.10 | all-reduce | flops 32 | bytes 256 | tf_op jit(solution)/shard_map/psum | solution.py:90
  346.0 75.9 %all-reduce.2.cloned.1.call-done = f32[32,2304]{1,0:T(8,128)} async-done(((f32[32,2304]{1,0:T(8,128)}), f32[32,2304]{1,0:T(8,128)}) %all-reduce.2.cloned.1.call-update) | async-done | bytes 294928 | tf_op jit(solution)/shard_map/psum | solution.py:90
  421.9 1.8 broadcast_divide_fusion
  (12 shorter events, 0.0 us)
Async XLA Ops:
  7.2 131.8 %copy-start = (bf16[1,480,2304]{2,1,0:T(8,128)(2,1)S(1)}, bf16[1,480,2304]{2,1,0:T(8,128)(2,1)}, u32[]{:S(2)}) copy-start(bf16[1,480,2304]{2,1,0:T(8,128)(2,1)} %param.13) | copy-start | bytes 6635524
  7.2 112.3 %all-gather.3.cloned.1.call-start = ((), (), s32[]{:S(2)}) async-start(), calls=%async_computation.5 | async-start | bytes 15925248 | tf_op jit(solution)/shard_map/all_gather | solution.py:64
  46.3 182.4 %reduce-scatter.2.cloned.1.call-start = ((), (), s32[]{:S(2)}) async-start(), calls=%async_computation.3 | async-start | bytes 15925248 | tf_op jit(solution)/shard_map/reduce_scatter | solution.py:66
  119.5 11.4 %copy-start.5 = (bf16[128,24,2304]{2,0,1:T(8,128)(2,1)S(1)}, bf16[128,24,2304]{2,0,1:T(8,128)(2,1)}, u32[]{:S(2)}) copy-start(bf16[128,24,2304]{2,0,1:T(8,128)(2,1)} %all-gather.3.cloned.1.call-done) | copy-start | bytes 42467332
  119.5 11.4 %copy-start.6 = (bf16[1,2304,480]{1,2,0:T(8,128)(2,1)S(1)}, bf16[1,2304,480]{1,2,0:T(8,128)(2,1)}, u32[]{:S(2)}) copy-start(bf16[1,2304,480]{1,2,0:T(8,128)(2,1)} %param.11) | copy-start | bytes 6635524
  232.0 7.1 %copy-start.2 = (s32[64,2]{0,1:T(2,128)S(1)}, s32[64,2]{0,1:T(2,128)}, u32[]{:S(2)}) copy-start(s32[64,2]{0,1:T(2,128)} %param.8) | copy-start | bytes 1540
  232.0 7.5 %copy-start.3 = (f32[64,2]{0,1:T(2,128)S(1)}, f32[64,2]{0,1:T(2,128)}, u32[]{:S(2)}) copy-start(f32[64,2]{0,1:T(2,128)} %param.9) | copy-start | bytes 1540
  232.0 30.9 %all-to-all-start.1 = ((bf16[16,1,24,2304]{3,2,1,0:T(8,128)(2,1)}), bf16[16,1,24,2304]{3,2,1,0:T(8,128)(2,1)}, u32[]{:S(2)}, u32[]{:S(2)}) async-start(bf16[16,1,24,2304]{3,2,1,0:T(8,128)(2,1)} %copy.37), calls=%async_computation.2 | async-start | bytes 3538944 | tf_op jit(solution)/shard_map/all_to_all | solution.py:74
  238.9 183.0 %all-reduce.2.cloned.1.call-start = ((), (), s32[]{:S(2)}) async-start(), calls=%async_computation.4 | async-start | bytes 589824 | tf_op jit(solution)/shard_map/psum | solution.py:90
  270.0 6.3 %copy-start.4 = (s32[64]{0:T(128)S(1)}, s32[64]{0:T(128)}, u32[]{:S(2)}) copy-start(s32[64]{0:T(128)} %param.10) | copy-start | bytes 772
  276.3 147.3 %copy-start.1 = (bf16[64,2304]{1,0:T(8,128)(2,1)}, bf16[64,2304]{1,0:T(8,128)(2,1)S(1)}, u32[]{:S(2)}) copy-start(bf16[64,2304]{1,0:T(8,128)(2,1)S(1)} %fusion.11) | copy-start | bytes 884740
Sparse Core Ops, SparseCore 0:
  46.5 72.9 all-gather.2
  149.4 79.3 reduce-scatter.1
  277.4 144.4 all-reduce.1
where the time goes:
time: 431 us; the launch traced here: 430 us
  waiting for transfers between devices  252 us (58%)
  blocking collectives  101 us (23%)
  matrix products  32 us (7%)
  between operations  13.9 us (3%)
  local copies, waits for them, and re-layouts  12.5 us (3%)
  other arithmetic  11.7 us (3%)
  starting transfers between devices  7.18 us (2%)
    reduce_scatter x1, waiting for transfers between devices, shards(): lax.psum_scatter(jnp.einsum('nacf,afd->nacd', hidden, w_down, preferred_e...  79.5 us
    psum x1, waiting for transfers between devices, shards(): lax.psum((seq_sums, seq_counts), ('dp', 'tensor', 'expert'))  75.9 us
    all_gather x1, waiting for transfers between devices, shards(): lax.all_gather(local_rows, ('dp', 'tensor'), axis=0, tiled=True)  73.1 us
    psum x1, blocking collectives, shards(): lax.psum((seq_sums, seq_counts), ('dp', 'tensor', 'expert'))  68.6 us
    all_to_all x1, blocking collectives, shards(): lax.all_to_all(send_rows, 'expert', split_axis=0, concat_axis=0, tiled=True)  32.4 us
    all_to_all x1, waiting for transfers between devices, shards(): lax.all_to_all(summed, 'expert', split_axis=0, concat_axis=0, tiled=True)  23.3 us
    dot_general x1, matrix products, expert_hidden(): jnp.einsum('nacd,adf->nacf', row_block, w_up, preferred_element_type=jnp....  11.4 us
    dot_general x1, matrix products, shards(): jnp.einsum('nacf,afd->nacd', hidden, w_down, preferred_element_type=jnp.f...  10.3 us
  transfers between devices with their start and end apart: 4, of which 4 were waited for; matrix products, arithmetic and copies ran while one was open for 0% of the time, Pallas kernels for 0%

commit v1 on v0

--- a/solution.py
+++ b/solution.py
@@ -61,7 +61,14 @@
     received = lax.all_to_all(send_rows, "expert", split_axis=0, concat_axis=0, tiled=True)
     local_rows = received.reshape(experts_axis, per_device, CAP, width)
     hidden = expert_hidden(
-        lax.all_gather(local_rows, ("dp", "tensor"), axis=0, tiled=True), w_gate, w_up
+        jnp.concatenate(
+            lax.all_to_all(
+                jnp.stack([local_rows] * lax.axis_size(("dp", "tensor"))), ("dp", "tensor"), 0, 0
+            ),
+            axis=0,
+        ),
+        w_gate,
+        w_up,
     )
     summed = lax.psum_scatter(
         jnp.einsum("nacf,afd->nacd", hidden, w_down, preferred_element_type=jnp.float32).astype(

time: 431 us -> 515 us (1.19)
  blocking collectives: 101 us -> 264 us
  waiting for transfers between devices: 252 us -> 175 us
    all_to_all x0 -> x1, blocking collectives: none -> 164 us  [shards(): lax.all_to_all(jnp.stack([local_rows] * lax.axis_size(('dp', 'tensor'))),...]
    all_gather x1 -> x0, waiting for transfers between devices: 73.1 us -> none  [shards(): lax.all_gather(local_rows, ('dp', 'tensor'), axis=0, tiled=True)]
  transfers between devices with their start and end apart: 4 -> 3, of which waited for: 4 -> 3; matrix products, arithmetic and copies ran while one was open for 0% -> 0% of each run, Pallas kernels for 0% -> 0%
where the time goes in v1:
time: 515 us; the launch traced here: 514 us
  blocking collectives  264 us (51%)
  waiting for transfers between devices  175 us (34%)
  matrix products  27.7 us (5%)
  local copies, waits for them, and re-layouts  14.5 us (3%)
  between operations  14.2 us (3%)
  other arithmetic  11.7 us (2%)
  starting transfers between devices  7.12 us (1%)
    all_to_all x1, blocking collectives, shards(): lax.all_to_all(jnp.stack([local_rows] * lax.axis_size(('dp', 'tensor'))),...  164 us
    psum x1, waiting for transfers between devices, shards(): lax.psum((seq_sums, seq_counts), ('dp', 'tensor', 'expert'))  75.9 us
    reduce_scatter x1, waiting for transfers between devices, shards(): lax.psum_scatter(jnp.einsum('nacf,afd->nacd', hidden, w_down, preferred_e...  75.4 us
    psum x1, blocking collectives, shards(): lax.psum((seq_sums, seq_counts), ('dp', 'tensor', 'expert'))  68.5 us
    all_to_all x1, blocking collectives, shards(): lax.all_to_all(send_rows, 'expert', split_axis=0, concat_axis=0, tiled=True)  32.4 us
    all_to_all x1, waiting for transfers between devices, shards(): lax.all_to_all(summed, 'expert', split_axis=0, concat_axis=0, tiled=True)  23.3 us
  transfers between devices with their start and end apart: 3, of which 3 were waited for; matrix products, arithmetic and copies ran while one was open for 0% of the time, Pallas kernels for 0%

profile of v1, /device:TPU:1, one launch (start us, length us, event | category | flops | bytes accessed | tf_op | source)
XLA Modules:
  0.0 514.4 jit_solution(14627796124889038940)
XLA Ops:
  7.2 0.0 copy-start
  7.2 0.0 reduce-scatter.2.cloned.1.call-start
  7.2 0.9 copy.35
  8.1 0.1 reshape.119
  8.3 0.1 fusion.14
  8.4 0.2 reduce_window_sum.11
  8.5 0.2 select_reduce_fusion
  8.7 0.1 reduce_sum.59
  8.9 0.1 copy.36
  8.9 0.7 compare_and_fusion
  9.6 0.1 convert_reduce_fusion.1
  9.7 1.1 fusion.9
  10.9 1.4 convolution_convert_fusion
  12.3 0.1 broadcast_in_dim.13
  12.4 32.4 %all_to_all.19 = bf16[16,24,2304]{2,1,0:T(8,128)(2,1)S(1)} all-to-all(bf16[16,24,2304]{2,1,0:T(8,128)(2,1)S(1)} %bitcast.66), channel_id=1, replica_groups=mesh['dp'=4,'tensor'=2,'expert'=16] {'expert'}, dimensions={0} | all-to-all | bytes 3538944 | tf_op jit(solution)/shard_map/all_to_all | solution.py:61
  44.8 0.3 copy.38
  45.1 1.2 stack.3
  46.3 163.6 %all_to_all.20 = bf16[8,16,1,24,2304]{4,1,3,2,0:T(8,128)(2,1)S(1)} all-to-all(bf16[8,16,1,24,2304]{4,1,3,2,0:T(8,128)(2,1)S(1)} %stack.3), channel_id=1, replica_groups=mesh['dp'=4,'tensor'=2,'expert'=16] {'dp','tensor'}, dimensions={0} | all-to-all | bytes 28311552 | tf_op jit(solution)/shard_map/all_to_all | solution.py:65
  209.9 1.9 copy.39
  211.8 0.0 copy-done.5
  211.9 0.0 copy-start.6
  211.9 7.0 %fusion.6 = f32[128,24,480]{0,2,1:T(8,128)S(1)} fusion(bf16[128,24,2304]{2,0,1:T(8,128)(2,1)S(1)} %bitcast.64, bf16[1,2304,480]{1,2,0:T(8,128)(2,1)S(1)} %copy-done.5), kind=kOutput, calls=%fused_computation.13 | convolution fusion | flops 6794772480 | bytes 22265856 | tf_op jit(solution)/shard_map/nacd,adf->nacf/dot_general | solution.py:45
  218.9 0.0 copy-done.6
  218.9 8.1 %fusion = bf16[128,1,24,480]{0,3,2,1:T(8,128)(2,1)S(1)} fusion(f32[128,24,480]{0,2,1:T(8,128)S(1)} %fusion.6, bf16[128,24,2304]{2,0,1:T(8,128)(2,1)S(1)} %bitcast.65, bf16[1,2304,480]{1,2,0:T(8,128)(2,1)S(1)} %copy-done.6), kind=kOutput, calls=%fused_computation.3 | convolution fusion | flops 6803619840 | bytes 25214976 | tf_op jit(solution)/shard_map/nacd,adf->nacf/dot_general | solution.py:44
  227.0 10.3 %convert_bitcast_fusion = bf16[128,1,24,2304]{3,0,2,1:T(8,128)(2,1)} fusion(bf16[128,1,24,480]{0,3,2,1:T(8,128)(2,1)S(1)} %fusion, bf16[1,480,2304]{2,1,0:T(8,128)(2,1)S(1)} %copy-done), kind=kOutput, calls=%fused_computation.1 | convolution fusion | flops 6801850368 | bytes 19316736 | tf_op jit(solution)/shard_map/nacf,afd->nacd/dot_general | solution.py:74
  237.3 0.0 reduce-scatter.2.cloned.1.call-update
  237.3 75.4 %reduce-scatter.2.cloned.1.call-done = bf16[16,1,24,2304]{3,0,2,1:T(8,128)(2,1)} async-done(((bf16[128,1,24,2304]{3,0,2,1:T(8,128)(2,1)}), bf16[16,1,24,2304]{3,0,2,1:T(8,128)(2,1)}) %reduce-scatter.2.cloned.1.call-update) | async-done | bytes 1769488 | tf_op jit(solution)/shard_map/reduce_scatter | solution.py:73
  312.7 3.2 copy.40
  315.9 6.9 %all-to-all-start.2 = ((bf16[16,1,24,2304]{3,2,1,0:T(8,128)(2,1)}), bf16[16,1,24,2304]{3,2,1,0:T(8,128)(2,1)}, u32[]{:S(2)}, u32[]{:S(2)}) async-start(bf16[16,1,24,2304]{3,2,1,0:T(8,128)(2,1)} %copy.40), calls=%async_computation.3 | async-start | bytes 3538944 | tf_op jit(solution)/shard_map/all_to_all | solution.py:81
  322.8 0.2 all-reduce.2.cloned.1.call-start
  323.0 0.1 copy.43
  323.1 0.1 mul.61
  323.3 0.1 copy.37
  323.4 0.1 copy.34
  323.5 23.3 %all-to-all-done.2 = bf16[16,1,24,2304]{3,2,1,0:T(8,128)(2,1)} async-done(((bf16[16,1,24,2304]{3,2,1,0:T(8,128)(2,1)}), bf16[16,1,24,2304]{3,2,1,0:T(8,128)(2,1)}, u32[]{:S(2)}, u32[]{:S(2)}) %all-to-all-start.2) | async-done | bytes 1769504 | tf_op jit(solution)/shard_map/all_to_all | solution.py:81
  346.9 3.2 convert_reduce_fusion
  350.0 4.0 gather_fusion
  354.0 2.0 gather.7
  356.0 3.2 multiply_reduce_fusion
  359.3 1.0 fusion.11
  360.3 0.0 copy-start.1
  360.3 0.9 fusion.17
  361.2 0.0 all-reduce.2.cloned.1.call-update
  361.2 0.1 convert_reduce_fusion.2
  361.3 68.5 %psum.15 = f32[32]{0:T(128)S(1)} all-reduce(f32[32]{0:T(128)S(1)} %convert_reduce_fusion.2), channel_id=1, replica_groups=mesh['dp'=4,'tensor'=2,'expert'=16] {'dp','tensor','expert'}, use_global_device_ids=true, to_apply=%region_9.10 | all-reduce | flops 32 | bytes 256 | tf_op jit(solution)/shard_map/psum | solution.py:97
  429.8 75.9 %all-reduce.2.cloned.1.call-done = f32[32,2304]{1,0:T(8,128)} async-done(((f32[32,2304]{1,0:T(8,128)}), f32[32,2304]{1,0:T(8,128)}) %all-reduce.2.cloned.1.call-update) | async-done | bytes 294928 | tf_op jit(solution)/shard_map/psum | solution.py:97
  505.7 1.8 broadcast_divide_fusion
  507.5 0.0 copy-done.1
  (12 shorter events, 0.0 us)
Async XLA Ops:
  7.2 219.8 %copy-start = (bf16[1,480,2304]{2,1,0:T(8,128)(2,1)S(1)}, bf16[1,480,2304]{2,1,0:T(8,128)(2,1)}, u32[]{:S(2)}) copy-start(bf16[1,480,2304]{2,1,0:T(8,128)(2,1)} %param.13) | copy-start | bytes 6635524
  7.2 305.5 %reduce-scatter.2.cloned.1.call-start = ((), (), s32[]{:S(2)}) async-start(), calls=%async_computation.4 | async-start | bytes 15925248 | tf_op jit(solution)/shard_map/reduce_scatter | solution.py:73
  209.9 1.9 copy-start.5
  211.9 7.1 %copy-start.6 = (bf16[1,2304,480]{1,2,0:T(8,128)(2,1)S(1)}, bf16[1,2304,480]{1,2,0:T(8,128)(2,1)}, u32[]{:S(2)}) copy-start(bf16[1,2304,480]{1,2,0:T(8,128)(2,1)} %param.11) | copy-start | bytes 6635524
  315.9 7.1 %copy-start.2 = (s32[64,2]{0,1:T(2,128)S(1)}, s32[64,2]{0,1:T(2,128)}, u32[]{:S(2)}) copy-start(s32[64,2]{0,1:T(2,128)} %param.8) | copy-start | bytes 1540
  315.9 7.5 %copy-start.3 = (f32[64,2]{0,1:T(2,128)S(1)}, f32[64,2]{0,1:T(2,128)}, u32[]{:S(2)}) copy-start(f32[64,2]{0,1:T(2,128)} %param.9) | copy-start | bytes 1540
  315.9 30.9 %all-to-all-start.2 = ((bf16[16,1,24,2304]{3,2,1,0:T(8,128)(2,1)}), bf16[16,1,24,2304]{3,2,1,0:T(8,128)(2,1)}, u32[]{:S(2)}, u32[]{:S(2)}) async-start(bf16[16,1,24,2304]{3,2,1,0:T(8,128)(2,1)} %copy.40), calls=%async_computation.3 | async-start | bytes 3538944 | tf_op jit(solution)/shard_map/all_to_all | solution.py:81
  322.8 183.0 %all-reduce.2.cloned.1.call-start = ((), (), s32[]{:S(2)}) async-start(), calls=%async_computation.5 | async-start | bytes 589824 | tf_op jit(solution)/shard_map/psum | solution.py:97
  354.0 6.3 %copy-start.4 = (s32[64]{0:T(128)S(1)}, s32[64]{0:T(128)}, u32[]{:S(2)}) copy-start(s32[64]{0:T(128)} %param.10) | copy-start | bytes 772
  360.3 147.2 %copy-start.1 = (bf16[64,2304]{1,0:T(8,128)(2,1)}, bf16[64,2304]{1,0:T(8,128)(2,1)S(1)}, u32[]{:S(2)}) copy-start(bf16[64,2304]{1,0:T(8,128)(2,1)S(1)} %fusion.11) | copy-start | bytes 884740
Sparse Core Ops, SparseCore 0:
  237.4 75.2 reduce-scatter.1
  361.4 144.3 all-reduce.1
